TPU v7x, 32 devices: a whole 2x2x4 slice. The times are simulated.
32 devices in a mesh: px: 4 (over x, core), py: 8 (over z, y).
Axes of the slice: x: 2, y: 2, z: 4, core: 2. Of those that a mesh axis runs over, the one named last changes fastest.
Arguments:
- theta: float32 [58, 64, 2048], P(None, 'px', 'py'), may hold values from 0.5 to 1.5
- vapor: float32 [58, 64, 2048], P(None, 'px', 'py'), may hold values from 0.1 to 1
- cloud: float32 [58, 64, 2048], P(None, 'px', 'py'), may hold values from 0 to 0.4
- divergence: float32 [58, 64, 2048], P(None, 'px', 'py'), may hold values from -6 to 6
- edge_weight: float32 [3, 64, 2048], P(None, 'px', 'py'), may hold values from 0.5 to 2
- inv_area: float32 [64, 2048], P('px', 'py'), may hold values from 0.7 to 1.4
- damping: float32 [3, 58], replicated, may hold values from 0.0005 to 0.004
- exner: float32 [58], replicated, may hold values from 0.6 to 1
- sat_scale: float32 [58], replicated, may hold values from 0.1 to 0.6
- layer_mass: float32 [58], replicated, may hold values from 0.02 to 0.1
- span_of: int32 [64, 2048], P('px', 'py'), may hold values from 0 to 32767, as said below
Outputs:
- theta_next: float32 [58, 64, 2048], P(None, 'px', 'py')
- vapor_next: float32 [58, 64, 2048], P(None, 'px', 'py')
- cloud_next: float32 [58, 64, 2048], P(None, 'px', 'py')
- divergence_next: float32 [58, 64, 2048], P(None, 'px', 'py')
- precip_spans: float32 [4, 32768], P('px', 'py')
Inputs may be any that keep to these rules, and one draw needn't show every extreme that they name: `span_of`: position p of px index a belongs to device p // 4096 of the py row of a. Within the 16 rows of one px index the entries are a permutation. The columns of one device take exactly 384 positions of every device of its row and 1024 more positions of one other device of that row, so each device receives exactly 4096 positions.
All inputs are finite; a program needn't handle non-finite values.
Results may differ from a plain program's by a relative error of at most 0.00002.
Values sent between devices are 32-bit elements; how exact they have to be, the bound alone decides.
A program may use at most 128 MiB of HBM per device.

v0:
```python
import jax
import jax.numpy as jnp
from jax import lax
from jax.sharding import PartitionSpec as P

NSAT = 2


LATENT = 0.5
QCRIT = 0.2
AUTO_RATE = 0.5


def extended(cells, sides, width):
    for axis, dim in sides:
        count = lax.axis_size(axis)
        head = lax.slice_in_dim(cells, 0, width, axis=dim)
        tail = lax.slice_in_dim(cells, cells.shape[dim] - width, cells.shape[dim], axis=dim)
        cells = jnp.concatenate(
            [
                lax.ppermute(tail, axis, [(i, (i + 1) % count) for i in range(count)]),
                cells,
                lax.ppermute(head, axis, [((i + 1) % count, i) for i in range(count)]),
            ],
            axis=dim,
        )
    return cells


def shifted(array_in, step_row, step_col):
    height = array_in.shape[-2]
    breadth = array_in.shape[-1]
    return array_in[
        ..., 1 + step_row : height - 1 + step_row, 1 + step_col : breadth - 1 + step_col
    ]


def laplace(values, weights, inverse):
    centre = shifted(values, 0, 0)
    summed = shifted(weights[0], 0, 0) * (shifted(values, 1, 0) - centre)
    summed = summed + shifted(weights[0], -1, 0) * (shifted(values, -1, 0) - centre)
    summed = summed + shifted(weights[1], 0, 0) * (shifted(values, 0, 1) - centre)
    summed = summed + shifted(weights[1], 0, -1) * (shifted(values, 0, -1) - centre)
    summed = summed + shifted(weights[2], 0, 0) * (shifted(values, -1, 1) - centre)
    summed = summed + shifted(weights[2], 1, -1) * (shifted(values, 1, -1) - centre)
    return shifted(inverse, 0, 0) * summed


def adjust(theta_dyn, vapor_dyn, cloud, exner, sat_scale, layer_mass):
    temper = theta_dyn * exner
    condensed = jnp.zeros_like(theta_dyn)
    for repeat in range(NSAT):
        warmed = temper + LATENT * condensed
        saturation = sat_scale * jnp.exp(warmed)
        excess = vapor_dyn - condensed - saturation
        slope = -1.0 - LATENT * saturation
        condensed = condensed - excess / slope
    condensed = jnp.maximum(condensed, -cloud)
    theta_next = theta_dyn + LATENT * condensed / exner
    vapor_next = vapor_dyn - condensed
    liquid = cloud + condensed
    rained = AUTO_RATE * jnp.maximum(liquid - QCRIT, 0.0)
    cloud_next = liquid - rained
    precip = jnp.sum(layer_mass * rained, axis=0)
    return (theta_next, vapor_next, cloud_next, precip)


def on_device(
    theta,
    vapor,
    cloud,
    divergence,
    edge_weight,
    inv_area,
    damping,
    exner,
    sat_scale,
    layer_mass,
    span_of,
):
    levels = theta.shape[0]
    row_count = theta.shape[1]
    across = theta.shape[2]
    columns = row_count * across
    stacked = 3 * levels
    fields = jnp.concatenate([theta, vapor, divergence], 0)
    geometry = jnp.concatenate([edge_weight, inv_area[None]], 0)
    combined = jnp.concatenate([fields, geometry], 0)
    padded = extended(combined, (("px", 1), ("py", 2)), 1)
    geometry_pad = padded[stacked:]
    lap_once = laplace(padded[:stacked], geometry_pad[:3], geometry_pad[3])
    lap_padded = extended(lap_once, (("px", 1), ("py", 2)), 1)
    second = laplace(lap_padded, geometry_pad[:3], geometry_pad[3])
    damped = fields - damping.reshape(stacked)[:, None, None] * second
    flat_state = damped.reshape(stacked, columns)
    flat_cloud = cloud.reshape(levels, columns)
    peers = lax.axis_size("py")
    capacity = columns // 4 + 3 * columns // (4 * peers)
    positions = span_of.reshape(columns)
    target = positions // columns
    local_slot = positions % columns
    onehot = (target[:, None] == jnp.arange(peers, dtype=jnp.int32)[None, :]).astype(jnp.int32)
    pair_rank = jnp.sum((jnp.cumsum(onehot, axis=0) - onehot) * onehot, axis=1)
    send_slot = target * capacity + pair_rank
    slot_source = (
        jnp.full((peers * capacity,), columns, jnp.int32)
        .at[send_slot]
        .set(jnp.arange(columns, dtype=jnp.int32))
    )
    slot_live = slot_source < columns
    slot_clip = jnp.minimum(slot_source, columns - 1)
    slot_value = jnp.where(
        slot_live, jnp.take(local_slot, slot_clip).astype(jnp.float32), float(columns)
    )
    labels = slot_value.reshape(1, peers, capacity)
    exner_col = exner[:, None]
    scale_col = sat_scale[:, None]
    mass_col = layer_mass[:, None]
    theta_next, vapor_next, cloud_next, rainfall = adjust(
        flat_state[:levels],
        flat_state[levels : 2 * levels],
        flat_cloud,
        exner_col,
        scale_col,
        mass_col,
    )
    rain_send = jnp.where(slot_live, jnp.take(rainfall, slot_clip), 0.0).reshape(1, peers, capacity)
    rain_in, labels_in = (
        lax.all_to_all(rain_send, "py", split_axis=1, concat_axis=1, tiled=True),
        lax.all_to_all(labels, "py", split_axis=1, concat_axis=1, tiled=True),
    )
    span_index = labels_in.reshape(-1).astype(jnp.int32)
    arrived_at = (
        jnp.zeros((columns,), jnp.int32)
        .at[span_index]
        .set(jnp.arange(span_index.shape[0], dtype=jnp.int32), mode="drop")
    )
    precip_local = jnp.take(rain_in.reshape(-1), arrived_at)
    theta_out = theta_next.reshape(levels, row_count, across)
    vapor_out = vapor_next.reshape(levels, row_count, across)
    cloud_out = cloud_next.reshape(levels, row_count, across)
    divergence_next = damped[2 * levels :]
    return (theta_out, vapor_out, cloud_out, divergence_next, precip_local[None, :])


def solution(mesh):
    placed = (
        P(None, "px", "py"),
        P(None, "px", "py"),
        P(None, "px", "py"),
        P(None, "px", "py"),
        P(None, "px", "py"),
        P("px", "py"),
        P(),
        P(),
        P(),
        P(),
        P("px", "py"),
    )
    return jax.shard_map(
        on_device,
        mesh=mesh,
        in_specs=placed,
        out_specs=(
            P(None, "px", "py"),
            P(None, "px", "py"),
            P(None, "px", "py"),
            P(None, "px", "py"),
            P("px", "py"),
        ),
        check_vma=False,
    )
```

profile of v0, /device:TPU:0, one launch (start us, length us, event | category | flops | bytes accessed | tf_op | source)
XLA Modules:
  0.0 309.3 jit_solution(1403073305776249958)
XLA Ops:
  0.7 1.6 constant_dynamic-update-slice_fusion.7
  2.7 0.3 copy-done.12
  3.1 1.2 copy-done.6
  4.6 0.5 collective-permute-start
  5.1 0.7 copy.40
  5.8 1.9 collective-permute-start.1
  7.8 2.3 reduce-window.6
  10.1 0.3 slice_reduce_fusion
  11.0 15.5 %scatter_custom_fusion = s32[11264]{0:T(1024)S(1)} fusion(s32[4096]{0:T(1024)S(1)} %bitcast.57, s32[4096]{0:T(1024)S(1)} %iota.14, s32[]{:T(128)} %constant.81.clone.1), kind=kCustom, calls=%fused_computation.106 | custom fusion | bytes 45060 | tf_op jit(solution)/shard_map/scatter | solution.py:108
  26.6 62.4 %gather_fusion = s32[11264]{0:T(1024)S(1)} fusion(s32[4096]{0:T(1024)S(1)} %get-tuple-element.43, s32[11264]{0:T(1024)S(1)} %fusion.39), kind=kCustom, calls=%fused_computation | custom fusion | bytes 135168 | tf_op jit(solution)/shard_map/jit(_take)/gather | solution.py:113
  89.0 0.7 convert_select_fusion
  89.6 6.6 %all-to-all-start = ((f32[1,8,1408]{2,0,1:T(1,128)}), f32[1,8,1408]{2,0,1:T(1,128)}, u32[]{:S(2)}, u32[]{:S(2)}) async-start(f32[1,8,1408]{2,0,1:T(1,128)} %bitcast.8), calls=%async_computation | async-start | bytes 90112 | tf_op jit(solution)/shard_map/all_to_all | solution.py:130
  96.3 1.1 copy.41
  97.4 1.1 copy.42
  98.5 0.7 pad_maximum_fusion
  99.2 2.7 fusion.49
  102.0 2.6 copy.43
  104.6 2.0 collective-permute-start.2
  106.6 2.5 copy.44
  109.2 2.7 collective-permute-start.3
  112.0 0.8 convert_element_type.26
  112.8 2.3 copy.45
  115.2 2.3 copy.46
  117.5 1.1 maximum_bitcast_fusion.2
  118.6 0.6 copy-done
  119.2 0.7 copy-done.1
  120.2 1.5 copy-done.7
  121.7 11.8 %fusion.21 = f32[174,16,256]{2,1,0:T(8,128)S(1)} fusion(f32[174,16,256]{2,1,0:T(8,128)S(1)} %copy-done.7, f32[178,18,1]{2,1,0:T(8,128)S(1)} %copy-done, f32[178,1,256]{2,1,0:T(1,128)S(1)} %copy.42, f32[178,16,256]{2,1,0:T(8,128)S(1)} %constant_dynamic-update-slice_fusion.3, f32[178,1,256]{2,1,0:T(1,128)S(1)} %copy.41, f32[178,18,1]{2,1,0:T(8,128)S(1)} %copy-done.1, ...), kind=kLoop, calls=%fused_computation.39 | loop fusion | flops 22806528 | bytes 9122848 | tf_op jit(solution)/shard_map/mul | solution.py:46
  133.5 1.6 copy-done.2
  135.4 0.7 collective-permute-start.5
  136.2 41.7 %scatter_custom_fusion.1 = s32[4096]{0:T(1024)S(1)} fusion(s32[11264]{0:T(1024)S(1)} %bitcast.54, s32[11264]{0:T(1024)S(1)} %iota.15, s32[]{:T(128)} %constant.80.clone.1), kind=kCustom, calls=%fused_computation.124 | custom fusion | bytes 16388 | tf_op jit(solution)/shard_map/scatter | solution.py:136
  178.3 2.5 pad_maximum_fusion.1
  180.7 2.0 fusion.50
  182.8 1.0 copy.57
  183.7 3.3 %collective-permute-start.6 = (f32[174,18,1]{0,1,2:T(8,128)S(1)}, f32[174,18,1]{0,1,2:T(8,128)S(1)}, u32[]{:S(2)}, u32[]{:S(2)}) collective-permute-start(f32[174,18,1]{0,1,2:T(8,128)S(1)} %copy.57), channel_id=1, source_target_pairs={{1,0},{2,1},{3,2},{4,3},{5,4},{6,5},{7,6},{0,7},{9,8},{10,9},{11,1... | collective-permute-start | bytes 37592 | tf_op jit(solution)/shard_map/ppermute | solution.py:23
  187.0 2.7 copy.59
  189.8 2.3 copy.58
  192.1 4.4 %collective-permute-done.7 = f32[174,18,1]{0,1,2:T(8,128)} collective-permute-done((f32[174,18,1]{0,1,2:T(8,128)S(1)}, f32[174,18,1]{0,1,2:T(8,128)}, u32[]{:S(2)}, u32[]{:S(2)}) %collective-permute-start.7) | collective-permute-done | bytes 12560 | tf_op jit(solution)/shard_map/ppermute | solution.py:21
  196.5 3.0 copy.60
  199.5 10.5 %fusion.5 = f32[174,16,256]{2,1,0:T(8,128)S(1)} fusion(f32[174,16,256]{2,1,0:T(8,128)} %copy-done.6, f32[174,16,256]{2,1,0:T(8,128)S(1)} %copy-done.3, f32[174,18,1]{2,1,0:T(8,128)} %copy.60, f32[174,1,256]{2,1,0:T(1,128)S(1)} %copy.52, f32[174,1,256]{2,1,0:T(1,128)S(1)} %copy.54, f32[174,18,1]{2,1,0:T(8,128)} %copy.58, f32[16,256]{1,0:T(8,128)S(1)} %get-tuple-element.41, ...), kind=kLoop, calls=%fused_computation.13 | loop fusion | flops 24231936 | bytes 9049240 | tf_op jit(solution)/shard_map/sub | solution.py:94
  210.1 2.4 multiply_reduce_fusion
  212.5 62.4 %gather_fusion.1 = f32[11264]{0:T(1024)S(1)} fusion(f32[4096]{0:T(1024)S(1)} %bitcast.45, s32[11264]{0:T(1024)S(1)} %fusion.39), kind=kCustom, calls=%fused_computation.1 | custom fusion | bytes 135168 | tf_op jit(solution)/shard_map/jit(_take)/gather | solution.py:127
  275.0 0.6 select_select_fusion
  275.6 3.3 %all-to-all-start.1 = ((f32[1,8,1408]{2,0,1:T(1,128)}), f32[1,8,1408]{2,0,1:T(1,128)S(1)}, u32[]{:S(2)}, u32[]{:S(2)}) async-start(f32[1,8,1408]{2,0,1:T(1,128)} %bitcast.11), calls=%async_computation.1 | async-start | bytes 90112 | tf_op jit(solution)/shard_map/all_to_all | solution.py:129
  278.9 3.3 %slice_subtract_fusion = (f32[58,16,256]{2,1,0:T(8,128)}, f32[58,16,256]{2,1,0:T(8,128)}, f32[58,16,256]{2,1,0:T(8,128)}) fusion(f32[58,16,256]{2,1,0:T(8,128)} %get-tuple-element.14, f32[174,16,256]{2,1,0:T(8,128)S(1)} %copy-done.5, f32[58]{0:T(128)S(1)} %copy-done.15, f32[58,16,256]{2,1,0:T(8,128)} %param.13), kind=kLoop, calls=%fused_computation.66 | loop fusion | flops 2138112 | bytes 6652136 | tf_op jit(solution)/shard_map/sub | solution.py:60
  282.3 3.4 %all-to-all-done.1 = f32[1,8,1408]{2,0,1:T(1,128)S(1)} async-done(((f32[1,8,1408]{2,0,1:T(1,128)}), f32[1,8,1408]{2,0,1:T(1,128)S(1)}, u32[]{:S(2)}, u32[]{:S(2)}) %all-to-all-start.1) | async-done | bytes 45088 | tf_op jit(solution)/shard_map/all_to_all | solution.py:129
  285.6 23.0 %gather_fusion.2 = f32[4096]{0:T(1024)S(1)} fusion(f32[11264]{0:T(1024)S(1)} %bitcast.46, s32[4096]{0:T(1024)S(1)} %fusion.45), kind=kCustom, calls=%fused_computation.2 | custom fusion | bytes 49152 | tf_op jit(solution)/shard_map/jit(_take)/gather | solution.py:138
  308.7 0.6 and_select_fusion.1
  (73 shorter events, 2.6 us)
Async XLA Ops:
  0.6 1.6 copy-start.9
  0.6 1.9 copy-start.10
  2.2 0.8 copy-start.12
  2.2 2.1 copy-start.13
  2.5 5.2 %copy-start.11 = (s32[16,256]{1,0:T(8,128)S(1)}, s32[16,256]{1,0:T(8,128)}, u32[]{:S(2)}) copy-start(s32[16,256]{1,0:T(8,128)} %param.21) | copy-start | bytes 49156
  2.7 1.6 copy-start.6
  4.6 91.7 %collective-permute-start = (f32[178,1,256]{2,0,1:T(8,128)S(1)}, f32[178,1,256]{2,0,1:T(8,128)}, u32[]{:S(2)}, u32[]{:S(2)}) collective-permute-start(f32[178,1,256]{2,0,1:T(8,128)S(1)} %copy.39), channel_id=1, source_target_pairs={{0,8},{8,16},{16,24},{24,0},{1,9},{9,17},{17,25},{25,1},{2,10},{10... | collective-permute-start | bytes 546824 | tf_op jit(solution)/shard_map/ppermute | solution.py:21
  5.8 91.6 %collective-permute-start.1 = (f32[178,1,256]{2,0,1:T(8,128)}, f32[178,1,256]{2,0,1:T(8,128)}, u32[]{:S(2)}, u32[]{:S(2)}) collective-permute-start(f32[178,1,256]{2,0,1:T(8,128)} %copy.40), channel_id=1, source_target_pairs={{8,0},{16,8},{24,16},{0,24},{9,1},{17,9},{25,17},{1,25},{10,2},{18... | collective-permute-start | bytes 546824 | tf_op jit(solution)/shard_map/ppermute | solution.py:23
  89.6 22.4 %all-to-all-start = ((f32[1,8,1408]{2,0,1:T(1,128)}), f32[1,8,1408]{2,0,1:T(1,128)}, u32[]{:S(2)}, u32[]{:S(2)}) async-start(f32[1,8,1408]{2,0,1:T(1,128)} %bitcast.8), calls=%async_computation | async-start | bytes 90112 | tf_op jit(solution)/shard_map/all_to_all | solution.py:130
  102.0 9.9 %copy-start.17 = (f32[58]{0:T(128)S(1)}, f32[58]{0:T(128)}, u32[]{:S(2)}) copy-start(f32[58]{0:T(128)} %param.20) | copy-start | bytes 700
  102.0 9.9 %copy-start.14 = (f32[3,58]{1,0:T(4,128)S(1)}, f32[3,58]{1,0:T(4,128)}, u32[]{:S(2)}) copy-start(f32[3,58]{1,0:T(4,128)} %param.17) | copy-start | bytes 2092
  104.6 8.3 %collective-permute-start.2 = (f32[178,18,1]{0,1,2:T(8,128)S(1)}, f32[178,18,1]{0,1,2:T(8,128)S(1)}, u32[]{:S(2)}, u32[]{:S(2)}) collective-permute-start(f32[178,18,1]{0,1,2:T(8,128)S(1)} %copy.43), channel_id=1, source_target_pairs={{0,1},{1,2},{2,3},{3,4},{4,5},{5,6},{6,7},{7,0},{8,9},{9,10},{10,1... | collective-permute-start | bytes 38456 | tf_op jit(solution)/shard_map/ppermute | solution.py:21
  109.2 6.0 %collective-permute-start.3 = (f32[178,18,1]{0,1,2:T(8,128)S(1)}, f32[178,18,1]{0,1,2:T(8,128)S(1)}, u32[]{:S(2)}, u32[]{:S(2)}) collective-permute-start(f32[178,18,1]{0,1,2:T(8,128)S(1)} %copy.44), channel_id=1, source_target_pairs={{1,0},{2,1},{3,2},{4,3},{5,4},{6,5},{7,6},{0,7},{9,8},{10,9},{11,1... | collective-permute-start | bytes 38456 | tf_op jit(solution)/shard_map/ppermute | solution.py:23
  117.5 1.7 copy-start
  117.5 2.4 copy-start.1
  119.9 1.8 copy-start.7
  133.5 1.6 copy-start.2
  135.3 42.5 %collective-permute-start.4 = (f32[174,1,256]{2,0,1:T(8,128)S(1)}, f32[174,1,256]{2,0,1:T(8,128)S(1)}, u32[]{:S(2)}, u32[]{:S(2)}) collective-permute-start(f32[174,1,256]{2,0,1:T(8,128)S(1)} %copy.51), channel_id=1, source_target_pairs={{8,0},{16,8},{24,16},{0,24},{9,1},{17,9},{25,17},{1,25},{10,2},{18... | collective-permute-start | bytes 534536 | tf_op jit(solution)/shard_map/ppermute | solution.py:23
  135.4 42.7 %collective-permute-start.5 = (f32[174,1,256]{2,0,1:T(8,128)S(1)}, f32[174,1,256]{2,0,1:T(8,128)S(1)}, u32[]{:S(2)}, u32[]{:S(2)}) collective-permute-start(f32[174,1,256]{2,0,1:T(8,128)S(1)} %copy.53), channel_id=1, source_target_pairs={{0,8},{8,16},{16,24},{24,0},{1,9},{9,17},{17,25},{25,1},{2,10},{10... | collective-permute-start | bytes 534536 | tf_op jit(solution)/shard_map/ppermute | solution.py:21
  183.7 6.0 %collective-permute-start.6 = (f32[174,18,1]{0,1,2:T(8,128)S(1)}, f32[174,18,1]{0,1,2:T(8,128)S(1)}, u32[]{:S(2)}, u32[]{:S(2)}) collective-permute-start(f32[174,18,1]{0,1,2:T(8,128)S(1)} %copy.57), channel_id=1, source_target_pairs={{1,0},{2,1},{3,2},{4,3},{5,4},{6,5},{7,6},{0,7},{9,8},{10,9},{11,1... | collective-permute-start | bytes 37592 | tf_op jit(solution)/shard_map/ppermute | solution.py:23
  187.0 12.5 %copy-start.3 = (f32[174,16,256]{2,1,0:T(8,128)S(1)}, f32[174,16,256]{2,1,0:T(8,128)}, u32[]{:S(2)}) copy-start(f32[174,16,256]{2,1,0:T(8,128)} %copy-done.2) | copy-start | bytes 8552452
  189.7 6.8 %collective-permute-start.7 = (f32[174,18,1]{0,1,2:T(8,128)S(1)}, f32[174,18,1]{0,1,2:T(8,128)}, u32[]{:S(2)}, u32[]{:S(2)}) collective-permute-start(f32[174,18,1]{0,1,2:T(8,128)S(1)} %copy.59), channel_id=1, source_target_pairs={{0,1},{1,2},{2,3},{3,4},{4,5},{5,6},{6,7},{7,0},{8,9},{9,10},{10,1... | collective-permute-start | bytes 37592 | tf_op jit(solution)/shard_map/ppermute | solution.py:21
  199.5 10.6 %copy-start.8 = (f32[58,16,256]{2,1,0:T(8,128)S(1)}, f32[58,16,256]{2,1,0:T(8,128)}, u32[]{:S(2)}) copy-start(f32[58,16,256]{2,1,0:T(8,128)} %param.13) | copy-start | bytes 2850820
  199.5 10.6 %copy-start.15 = (f32[58]{0:T(128)S(1)}, f32[58]{0:T(128)}, u32[]{:S(2)}) copy-start(f32[58]{0:T(128)} %param.18) | copy-start | bytes 700
  199.5 10.6 %copy-start.16 = (f32[58]{0:T(128)S(1)}, f32[58]{0:T(128)}, u32[]{:S(2)}) copy-start(f32[58]{0:T(128)} %param.19) | copy-start | bytes 700
  210.1 2.4 copy-start.4
  212.5 66.4 %copy-start.5 = (f32[174,16,256]{2,1,0:T(8,128)S(1)}, f32[174,16,256]{2,1,0:T(8,128)}, u32[]{:S(2)}) copy-start(f32[174,16,256]{2,1,0:T(8,128)} %copy-done.4) | copy-start | bytes 8552452
  275.6 10.1 %all-to-all-start.1 = ((f32[1,8,1408]{2,0,1:T(1,128)}), f32[1,8,1408]{2,0,1:T(1,128)S(1)}, u32[]{:S(2)}, u32[]{:S(2)}) async-start(f32[1,8,1408]{2,0,1:T(1,128)} %bitcast.11), calls=%async_computation.1 | async-start | bytes 90112 | tf_op jit(solution)/shard_map/all_to_all | solution.py:129
where the time goes:
time: 310 us; the launch traced here: 309 us
  local copies, waits for them, and re-layouts  241 us (78%)
  other arithmetic  38 us (12%)
  starting transfers between devices  21.3 us (7%)
  waiting for transfers between devices  7.75 us (2%)
    gather x1, local copies, waits for them, and re-layouts, on_device(): jnp.take(local_slot, slot_clip).astype(jnp.float32)  62.4 us
    gather x1, local copies, waits for them, and re-layouts, on_device(): jnp.take(rainfall, slot_clip)  62.4 us
    scatter x1, local copies, waits for them, and re-layouts, on_device(): arrived_at = jnp.zeros((columns,), jnp.int32).at[span_index].set(jnp.aran...  41.7 us
    gather x1, local copies, waits for them, and re-layouts, on_device(): precip_local = jnp.take(rain_in.reshape(-1), arrived_at)  23 us
    scatter x1, local copies, waits for them, and re-layouts, on_device(): slot_source = jnp.full((peers * capacity,), columns, jnp.int32).at[send_s...  15.5 us
    mul x1, other arithmetic, laplace(): return shifted(inverse, 0, 0) * summed  11.8 us
    sub x1, other arithmetic, on_device(): damped = fields - damping.reshape(stacked)[:, None, None] * second  10.5 us
    slice x6, local copies, waits for them, and re-layouts, extended(): head = lax.slice_in_dim(cells, 0, width, axis=dim)  8.98 us
  transfers between devices with their start and end apart: 10, of which 2 were waited for; matrix products, arithmetic and copies ran while one was open for 47% of the time, Pallas kernels for 0%

commit v1 on v0

v1 whole, which is shorter than its diff:
```python
import functools

import jax
import jax.numpy as jnp
from jax import lax
from jax.experimental import pallas as pl
from jax.experimental.pallas import tpu as pltpu
from jax.sharding import PartitionSpec as P

NSAT = 2
LATENT = 0.5
QCRIT = 0.2
AUTO_RATE = 0.5

MESH = pl.DeviceIdType.MESH
LANES = 128
SUB = 8
CORNERS = ((1, 1), (1, -1), (-1, 1), (-1, -1))


def kernel(
    dims,
    theta,
    vapor,
    divergence,
    cloud,
    edge_weight,
    inv_area,
    span_of,
    damping,
    exner,
    sat_scale,
    layer_mass,
    theta_out,
    vapor_out,
    cloud_out,
    divergence_out,
    precip_out,
    nat,
    out,
    grid,
    lap,
    coef,
    consts,
    weights,
    areas,
    spans,
    col_send,
    col_recv,
    corner_send,
    corner_recv,
    high,
    low,
    rain_send,
    rain_recv,
    in_sem,
    out_sem,
    send_sem,
    recv_sem,
    rain_send_sem,
    rain_recv_sem,
):
    n_px, n_py, levels, rows, cols = dims
    pad = consts.shape[1]
    halves = cols // LANES
    groups = 3 * pad // SUB
    wide = cols + LANES
    block = rows * cols // LANES
    px = lax.axis_index("px")
    py = lax.axis_index("py")
    used = levels * rows

    def device(dx, dy):
        return (lax.rem(px + dx + n_px, n_px), lax.rem(py + dy + n_py, n_py))

    loads = []
    for f, source in enumerate((theta, vapor, divergence, cloud)):
        for h in range(halves):
            loads.append(
                pltpu.make_async_copy(
                    source.at[:, pl.ds(h * LANES, LANES)],
                    nat.at[f, h, pl.ds(0, used), :],
                    in_sem.at[len(loads)],
                )
            )
    for source, target in ((edge_weight, weights), (inv_area, areas), (span_of, spans)):
        loads.append(pltpu.make_async_copy(source, target, in_sem.at[len(loads)]))
    for load in loads:
        load.start()

    barrier = pltpu.get_barrier_semaphore()
    greeted = [(1, 0), (-1, 0)] + list(CORNERS) + [(0, d) for d in range(1, n_py)]
    for dx, dy in greeted:
        pl.semaphore_signal(barrier, inc=1, device_id=device(dx, dy), device_id_type=MESH)

    def fill(level, carry):
        at = pl.ds(level, 1)
        for k in range(3):
            consts[k, at, :] = jnp.full((1, LANES), damping[k, level], jnp.float32)
        consts[3, at, :] = jnp.full((1, LANES), exner[level], jnp.float32)
        consts[4, at, :] = jnp.full((1, LANES), sat_scale[level], jnp.float32)
        consts[5, at, :] = jnp.full((1, LANES), layer_mass[level], jnp.float32)
        return carry

    for k in range(6):
        start = levels // SUB * SUB
        consts[k, pl.ds(start, pad - start), :] = jnp.full(
            (pad - start, LANES), 1.0 if k == 3 else 0.0, jnp.float32
        )
    lax.fori_loop(0, levels, fill, 0)
    consts[6] = LATENT / consts[3]
    for f in range(4):
        for h in range(halves):
            nat[f, h, pl.ds(used, (pad - levels) * rows), :] = jnp.zeros(
                ((pad - levels) * rows, LANES), jnp.float32
            )

    for k in list(range(3 * halves)) + [4 * halves, 4 * halves + 1]:
        loads[k].wait()

    def turn(i):
        for f in range(3):
            for h in range(halves):
                grid[i + 2, pl.ds(f * pad, pad), pl.ds(h * LANES, LANES)] = nat[
                    f, h, pl.ds(i, pad, stride=rows), :
                ]
        for k in range(3):
            grid[i + 2, pl.ds(levels + k, 1), pl.ds(0, cols)] = weights[k, pl.ds(i, 1), :]
        grid[i + 2, pl.ds(levels + 3, 1), pl.ds(0, cols)] = areas[pl.ds(i, 1), :]

    def turn_edge(n, carry):
        turn(n + n // 2 * (rows - 4))
        return carry

    lax.fori_loop(0, 4, turn_edge, 0)
    pl.semaphore_wait(barrier, len(greeted))

    sends = []

    def send(source, target, to):
        k = len(sends)
        copy = pltpu.make_async_remote_copy(
            src_ref=source,
            dst_ref=target,
            send_sem=send_sem.at[k],
            recv_sem=recv_sem.at[k],
            device_id=to,
            device_id_type=MESH,
        )
        copy.start()
        sends.append(copy)

    def send_rows(first, count):
        part = pl.ds(first, count)
        lanes = pl.ds(0, cols)
        send(grid.at[pl.ds(rows, 2), part, lanes], grid.at[pl.ds(0, 2), part, lanes], device(1, 0))
        send(
            grid.at[pl.ds(2, 2), part, lanes],
            grid.at[pl.ds(rows + 2, 2), part, lanes],
            device(-1, 0),
        )

    send_rows(0, 2 * pad)

    def turn_inner(n, carry):
        turn(n + 2)
        return carry

    lax.fori_loop(0, rows - 4, turn_inner, 0)

    lane = lax.broadcasted_iota(jnp.int32, (SUB, LANES), 1)
    per = LANES // (2 * rows)

    def edge_tile(r, g, dy):
        first = cols - LANES if dy > 0 else 0
        return grid[r, pl.ds(pl.multiple_of(g * SUB, SUB), SUB), pl.ds(first, LANES)]

    def pack(q, carry):
        for side, dy in enumerate((1, -1)):
            packed = jnp.zeros((SUB, LANES), jnp.float32)
            for part in range(per):
                for i in range(rows):
                    p = (part * rows + i) * 2
                    shift = (p - (LANES - 2 if dy > 0 else 0)) % LANES
                    moved = edge_tile(i + 2, q * per + part, dy)
                    if shift:
                        moved = pltpu.roll(moved, shift, 1)
                    packed = jnp.where(lane // 2 == p // 2, moved, packed)
            col_send[side, pl.ds(pl.multiple_of(q * SUB, SUB), SUB), :] = packed
        return carry

    lax.fori_loop(0, groups // per, pack, 0)
    send(col_send.at[0], col_recv.at[0], device(0, 1))
    send(col_send.at[1], col_recv.at[1], device(0, -1))

    def pack_corner(g, carry):
        result = []
        for (dx, dy), packed in zip(CORNERS, carry):
            for k in range(2):
                p = 4 * g + 2 * k
                moved = edge_tile((rows if dx > 0 else 2) + k, g, dy)
                moved = pltpu.roll(moved, lax.rem(p + (2 if dy > 0 else 0), LANES), 1)
                packed = jnp.where(lane // 2 == 2 * g + k, moved, packed)
            result.append(packed)
        return tuple(result)

    packed = lax.fori_loop(
        0, groups, pack_corner, tuple(jnp.zeros((SUB, LANES), jnp.float32) for _ in CORNERS)
    )
    for k, (dx, dy) in enumerate(CORNERS):
        corner_send[k] = packed[k]
        send(corner_send.at[k], corner_recv.at[k], device(dx, dy))
    send_rows(2 * pad, pad)

    loads[4 * halves + 2].wait()
    high_count = high.shape[0]

    def upper(i, carry):
        place = spans[pl.ds(i, 1), :] // LANES
        rank = lax.broadcasted_iota(jnp.int32, (high_count, cols), 0)
        hit = jnp.where(rank == place, 1.0, 0.0).astype(jnp.bfloat16)
        high[:, pl.ds(pl.multiple_of(i * cols, cols), cols)] = hit
        return carry

    lax.fori_loop(0, rows, upper, 0)

    sends[2].wait_recv()
    sends[3].wait_recv()

    def unpack(q, carry):
        at = pl.ds(pl.multiple_of(q * SUB, SUB), SUB)
        from_left = col_recv[0, at, :]
        from_right = col_recv[1, at, :]
        for part in range(per):
            for i in range(rows):
                p = (part * rows + i) * 2
                left = pltpu.roll(from_left, (LANES - 2 - p) % LANES, 1) if p != LANES - 2 else from_left
                right = pltpu.roll(from_right, (LANES - p) % LANES, 1) if p else from_right
                g = q * per + part
                grid[i + 2, pl.ds(pl.multiple_of(g * SUB, SUB), SUB), pl.ds(cols, LANES)] = jnp.where(
                    lane < 64, right, left
                )
        return carry

    lax.fori_loop(0, groups // per, unpack, 0)

    def laplace_at(source, r, at, c):
        up = source[r + 1, at, :]
        mid = source[r, at, :]
        down = source[r - 1, at, :]
        from_right = c[3] * mid + c[4] * down
        from_left = c[5] * mid + c[6] * up
        return (
            (c[0] * up + c[1] * down)
            + c[2] * mid
            + pltpu.roll(from_right, wide - 1, 1)
            + pltpu.roll(from_left, 1, 1)
        )

    def geometry(r, k):
        return jnp.broadcast_to(grid[r, pl.ds(levels + k, 1), :], (SUB, wide))

    def first_laplace(r):
        area = geometry(r, 3)
        area_right = pltpu.roll(area, wide - 1, 1)
        ahead = area * geometry(r, 0)
        behind = area * geometry(r - 1, 0)
        to_right = area * geometry(r, 1)
        to_right_behind = area * geometry(r, 2)
        own = geometry(r, 1)
        ahead_own = geometry(r + 1, 2)
        to_left = area_right * own
        to_left_ahead = area_right * ahead_own
        centre = -(
            ahead
            + behind
            + to_right
            + to_right_behind
            + pltpu.roll(to_left, 1, 1)
            + pltpu.roll(to_left_ahead, 1, 1)
        )
        c = (
            ahead,
            behind,
            centre,
            pltpu.roll(to_right, 1, 1),
            pltpu.roll(to_right_behind, 1, 1),
            to_left,
            to_left_ahead,
        )
        for k in range(7):
            coef[r, k] = c[k]

        def step(q, carry):
            for k in range(2):
                at = pl.ds(pl.multiple_of((q * 2 + k) * SUB, SUB), SUB)
                lap[r, at, :] = laplace_at(grid, r, at, c)
            return carry

        lax.fori_loop(0, groups // 2, step, 0)

    def coefficients(r):
        return tuple(coef[r, k] for k in range(7))

    def spread(k, at):
        tile = consts[k, at, :]
        return jnp.concatenate([tile] * halves, axis=1)

    def damped(f, r, q, c):
        at = pl.ds(pl.multiple_of(f * pad + q * SUB, SUB), SUB)
        del4 = laplace_at(lap, r, at, c)[:, :cols]
        here = pl.ds(pl.multiple_of(q * SUB, SUB), SUB)
        return grid[r, at, pl.ds(0, cols)] - spread(f, here) * del4

    def put(k, r, q, value):
        for h in range(halves):
            out[k, h, pl.ds(q * (SUB * rows) + r - 2, SUB, stride=rows), :] = value[
                :, h * LANES : (h + 1) * LANES
            ]

    def physics(r):
        c = coefficients(r)

        def step(q, rain):
            here = pl.ds(pl.multiple_of(q * SUB, SUB), SUB)
            theta_dyn = damped(0, r, q, c)
            vapor_dyn = damped(1, r, q, c)
            cloud_now = jnp.concatenate(
                [
                    nat[3, h, pl.ds(q * (SUB * rows) + r - 2, SUB, stride=rows), :]
                    for h in range(halves)
                ],
                axis=1,
            )
            temper = theta_dyn * spread(3, here)
            scale = spread(4, here)
            condensed = jnp.zeros_like(temper)
            for repeat in range(NSAT):
                warmed = temper + LATENT * condensed if repeat else temper
                saturation = scale * jnp.exp(warmed)
                excess = vapor_dyn - condensed - saturation
                condensed = condensed + excess / (1.0 + LATENT * saturation)
            condensed = jnp.maximum(condensed, -cloud_now)
            put(0, r, q, theta_dyn + condensed * spread(6, here))
            put(1, r, q, vapor_dyn - condensed)
            liquid = cloud_now + condensed
            rained = AUTO_RATE * jnp.maximum(liquid - QCRIT, 0.0)
            put(2, r, q, liquid - rained)
            return rain + spread(5, here) * rained

        rain = lax.fori_loop(0, pad // SUB, step, jnp.zeros((SUB, cols), jnp.float32))
        total = jnp.sum(rain, axis=0, keepdims=True)
        place = lax.rem(spans[pl.ds(r - 2, 1), :], LANES)
        rank = lax.broadcasted_iota(jnp.int32, (LANES, cols), 0)
        head = total.astype(jnp.bfloat16).astype(jnp.float32)
        at = pl.ds(pl.multiple_of((r - 2) * cols, cols), cols)
        for k, piece in enumerate((head, total - head)):
            low[pl.ds(k * LANES, LANES), at] = jnp.where(rank == place, piece, 0.0).astype(
                jnp.bfloat16
            )

    def loop(lower, upper_end, do):
        def step(r, carry):
            do(r)
            return carry

        lax.fori_loop(lower, upper_end, step, 0)

    loop(3, rows + 1, first_laplace)
    for h in range(halves):
        loads[3 * halves + h].wait()
    loop(4, rows, physics)

    for k in (0, 1, 4, 5, 6, 7, 8, 9):
        sends[k].wait_recv()

    def unpack_corner(g, carry):
        at = pl.ds(pl.multiple_of(g * SUB, SUB), SUB)
        for dx in (1, -1):
            for k in range(2):
                p = 4 * g + 2 * k
                left = corner_recv[CORNERS.index((dx, 1))]
                right = corner_recv[CORNERS.index((dx, -1))]
                left = pltpu.roll(left, lax.rem(2 * LANES - 2 - p, LANES), 1)
                right = pltpu.roll(right, lax.rem(LANES - p, LANES), 1)
                r = k if dx > 0 else rows + 2 + k
                grid[r, at, pl.ds(cols, LANES)] = jnp.where(lane < 64, right, left)
        return carry

    lax.fori_loop(0, groups, unpack_corner, 0)
    loop(0, 4, lambda n: first_laplace(n + 1 + n // 2 * (rows - 2)))
    loop(0, 4, lambda n: physics(n + 2 + n // 2 * (rows - 4)))

    both = lax.dot_general(
        high[...],
        low[...],
        (((1,), (1,)), ((), ())),
        preferred_element_type=jnp.float32,
    )
    rain_send[...] = both[:, :LANES] + both[:, LANES:]
    rains = []
    for d in range(1, n_py):
        to = device(0, d)
        copy = pltpu.make_async_remote_copy(
            src_ref=rain_send.at[pl.ds(pl.multiple_of(to[1] * block, block), block), :],
            dst_ref=rain_recv.at[d - 1],
            send_sem=rain_send_sem.at[d - 1],
            recv_sem=rain_recv_sem.at[d - 1],
            device_id=to,
            device_id_type=MESH,
        )
        copy.start()
        rains.append(copy)

    stores = []

    def store(k, target):
        for h in range(halves):
            copy = pltpu.make_async_copy(
                out.at[k, h, pl.ds(0, used), :],
                target.at[:, pl.ds(h * LANES, LANES)],
                out_sem.at[len(stores)],
            )
            copy.start()
            stores.append(copy)

    store(0, theta_out)
    store(1, vapor_out)
    store(2, cloud_out)

    def diverge(r):
        c = coefficients(r)

        def step(q, carry):
            put(3, r, q, damped(2, r, q, c))
            return carry

        lax.fori_loop(0, pad // SUB, step, 0)

    loop(2, rows + 2, diverge)
    store(3, divergence_out)

    total = rain_send[pl.ds(pl.multiple_of(py * block, block), block), :]
    for d in range(1, n_py):
        rains[d - 1].wait_recv()
        total = total + rain_recv[d - 1]
    precip_out[...] = total
    for copy in sends:
        copy.wait_send()
    for copy in rains:
        copy.wait_send()
    for copy in stores:
        copy.wait()


def on_device(
    n_px,
    n_py,
    theta,
    vapor,
    cloud,
    divergence,
    edge_weight,
    inv_area,
    damping,
    exner,
    sat_scale,
    layer_mass,
    span_of,
):
    levels, rows, cols = theta.shape
    pad = (levels + 4 + SUB - 1) // SUB * SUB
    halves = cols // LANES
    wide = cols + LANES
    block = rows * cols // LANES
    flat = jax.ShapeDtypeStruct((levels * rows, cols), jnp.float32)
    f32 = jnp.float32
    anywhere = pl.BlockSpec(memory_space=pl.ANY)
    scalars = pl.BlockSpec(memory_space=pltpu.SMEM)
    theta_next, vapor_next, cloud_next, divergence_next, precip = pl.pallas_call(
        functools.partial(kernel, (n_px, n_py, levels, rows, cols)),
        out_shape=(flat, flat, flat, flat, jax.ShapeDtypeStruct((block, LANES), f32)),
        in_specs=[anywhere] * 7 + [scalars] * 4,
        out_specs=(anywhere,) * 4 + (pl.BlockSpec(memory_space=pltpu.VMEM),),
        scratch_shapes=[
            pltpu.VMEM((4, halves, pad * rows, LANES), f32),
            pltpu.VMEM((4, halves, pad * rows, LANES), f32),
            pltpu.VMEM((rows + 4, 3 * pad, wide), f32),
            pltpu.VMEM((rows + 4, 3 * pad, wide), f32),
            pltpu.VMEM((rows + 4, 7, SUB, wide), f32),
            pltpu.VMEM((7, pad, LANES), f32),
            pltpu.VMEM((3, rows, cols), f32),
            pltpu.VMEM((rows, cols), f32),
            pltpu.VMEM((rows, cols), jnp.int32),
            pltpu.VMEM((2, 3 * pad * 2 * rows // LANES, LANES), f32),
            pltpu.VMEM((2, 3 * pad * 2 * rows // LANES, LANES), f32),
            pltpu.VMEM((4, SUB, LANES), f32),
            pltpu.VMEM((4, SUB, LANES), f32),
            pltpu.VMEM((n_py * block, rows * cols), jnp.bfloat16),
            pltpu.VMEM((2 * LANES, rows * cols), jnp.bfloat16),
            pltpu.VMEM((n_py * block, LANES), f32),
            pltpu.VMEM((n_py - 1, block, LANES), f32),
            pltpu.SemaphoreType.DMA((4 * halves + 3,)),
            pltpu.SemaphoreType.DMA((4 * halves,)),
            pltpu.SemaphoreType.DMA((10,)),
            pltpu.SemaphoreType.DMA((10,)),
            pltpu.SemaphoreType.DMA((n_py - 1,)),
            pltpu.SemaphoreType.DMA((n_py - 1,)),
        ],
        compiler_params=pltpu.CompilerParams(
            collective_id=0, has_side_effects=True, vmem_limit_bytes=48 * 1024 * 1024
        ),
        cost_estimate=pl.CostEstimate(
            flops=60 * levels * rows * cols, bytes_accessed=32 * levels * rows * cols, transcendentals=0
        ),
    )(
        theta.reshape(levels * rows, cols),
        vapor.reshape(levels * rows, cols),
        divergence.reshape(levels * rows, cols),
        cloud.reshape(levels * rows, cols),
        edge_weight,
        inv_area,
        span_of,
        damping,
        exner,
        sat_scale,
        layer_mass,
    )
    shape = (levels, rows, cols)
    return (
        theta_next.reshape(shape),
        vapor_next.reshape(shape),
        cloud_next.reshape(shape),
        divergence_next.reshape(shape),
        precip.reshape(1, block * LANES),
    )


def solution(mesh):
    placed = (
        P(None, "px", "py"),
        P(None, "px", "py"),
        P(None, "px", "py"),
        P(None, "px", "py"),
        P(None, "px", "py"),
        P("px", "py"),
        P(),
        P(),
        P(),
        P(),
        P("px", "py"),
    )
    return jax.shard_map(
        functools.partial(on_device, mesh.shape["px"], mesh.shape["py"]),
        mesh=mesh,
        in_specs=placed,
        out_specs=(
            P(None, "px", "py"),
            P(None, "px", "py"),
            P(None, "px", "py"),
            P(None, "px", "py"),
            P("px", "py"),
        ),
        check_vma=False,
    )
```

time: 310 us -> 77.1 us (0.25)
  local copies, waits for them, and re-layouts: 241 us -> 9.62 us
  Pallas kernels: 0 us -> 66.3 us
  other arithmetic: 38 us -> 0 us
  starting transfers between devices: 21.3 us -> 0 us
  waiting for transfers between devices: 7.75 us -> 0 us
    gather x3 -> x0, local copies, waits for them, and re-layouts: 148 us -> none  [the longest x1 62.4 us: on_device(): jnp.take(local_slot, slot_clip).astype(jnp.float32)]
    pallas_call x0 -> x1, Pallas kernels: none -> 66.3 us  [on_device(): pl.pallas_call(functools.partial(kernel, (n_px, n_py, levels, rows, cols)...]
    scatter x2 -> x0, local copies, waits for them, and re-layouts: 57.2 us -> none  [the longest x1 41.7 us: on_device(): arrived_at = jnp.zeros((columns,), jnp.int32).at[span_index].set(jnp.aran...]
    slice x16 -> x0, local copies, waits for them, and re-layouts: 15.3 us -> none  [the longest x6 8.98 us: extended(): head = lax.slice_in_dim(cells, 0, width, axis=dim)]
    sub x2 -> x0, other arithmetic: 13.9 us -> none  [the longest x1 10.5 us: on_device(): damped = fields - damping.reshape(stacked)[:, None, None] * second]
    ppermute x8 -> x0, local copies, waits for them, and re-layouts: 12.6 us -> none  [the longest x4 6.65 us: extended(): lax.ppermute(tail, axis, [(i, (i + 1) % count) for i in range(count)])]
    mul x2 -> x0, other arithmetic: 11.8 us -> none  [the longest x1 11.8 us: laplace(): return shifted(inverse, 0, 0) * summed]
    ppermute x8 -> x0, starting transfers between devices: 11.3 us -> none  [the longest x4 8.02 us: extended(): lax.ppermute(head, axis, [((i + 1) % count, i) for i in range(count)])]
  transfers between devices with their start and end apart: 10 -> 0, of which waited for: 2 -> 0; matrix products, arithmetic and copies ran while one was open for 47% -> 0% of each run, Pallas kernels for 0% -> 0%
where the time goes in v1:
time: 77.1 us; the launch traced here: 76.7 us
  Pallas kernels  66.3 us (86%)
  local copies, waits for them, and re-layouts  9.62 us (12%)
    pallas_call x1, Pallas kernels, on_device(): pl.pallas_call(functools.partial(kernel, (n_px, n_py, levels, rows, cols)...  66.3 us
    unnamed x23, local copies, waits for them, and re-layouts  9.62 us

profile of v1, /device:TPU:0, one launch (start us, length us, event | category | flops | bytes accessed | tf_op | source)
XLA Modules:
  0.0 76.7 jit_solution(13671842271274965625)
XLA Ops:
  0.6 0.0 copy-start.5
  0.6 0.0 copy-start.6
  0.7 0.0 copy-start.7
  0.7 0.0 copy-start.8
  0.7 0.6 copy-done.5
  1.3 0.0 copy-done.6
  1.3 0.0 copy-done.7
  1.3 0.0 copy-done.8
  1.3 0.0 copy-start
  1.3 1.2 %copy-done = f32[58,16,256]{2,1,0:T(8,128)S(1)} copy-done((f32[58,16,256]{2,1,0:T(8,128)S(1)}, f32[58,16,256]{2,1,0:T(8,128)}, u32[]{:S(2)}) %copy-start) | copy-done | bytes 950296
  2.5 0.0 copy-start.1
  2.5 1.2 %copy-done.1 = f32[58,16,256]{2,1,0:T(8,128)S(1)} copy-done((f32[58,16,256]{2,1,0:T(8,128)S(1)}, f32[58,16,256]{2,1,0:T(8,128)}, u32[]{:S(2)}) %copy-start.1) | copy-done | bytes 950296
  3.7 0.0 copy-start.2
  3.7 0.8 %copy-done.2 = f32[3,16,256]{2,1,0:T(8,128)S(1)} copy-done((f32[3,16,256]{2,1,0:T(8,128)S(1)}, f32[3,16,256]{2,1,0:T(8,128)}, u32[]{:S(2)}) %copy-start.2) | copy-done | bytes 49176
  4.5 0.0 copy-start.3
  4.5 0.7 copy-done.3
  5.2 0.0 copy-start.4
  5.2 0.7 copy-done.4
  6.0 66.3 %shard_map.146 = (f32[928,256]{1,0:T(8,128)S(1)}, f32[928,256]{1,0:T(8,128)S(1)}, f32[928,256]{1,0:T(8,128)S(1)}, f32[928,256]{1,0:T(8,128)S(1)}, f32[32,128]{1,0:T(8,128)S(1)}) custom-call(f32[928,256]{1,0:T(8,128)S(1)} %bitcast.9, f32[928,256]{1,0:T(8,128)S(1)} %bitcast.10, f32[928,256]{1,0:T(8,128)} %bitcast.16, f32[928,256]{1,0:T(8,128)} %bitcast.17, ...), custom_call_target="tpu_custom_call" | custom-call | flops 14254080 | bytes 7602176 | tf_op jit(solution)/shard_map/pallas_call | solution.py:480
  72.3 0.9 %copy.21 = f32[58,16,256]{2,1,0:T(8,128)} copy(f32[58,16,256]{2,1,0:T(8,128)S(1)} %bitcast.14) | data formatting | bytes 1900544
  73.3 0.9 %copy.22 = f32[58,16,256]{2,1,0:T(8,128)} copy(f32[58,16,256]{2,1,0:T(8,128)S(1)} %bitcast.13) | data formatting | bytes 1900544
  74.2 0.9 %copy.23 = f32[58,16,256]{2,1,0:T(8,128)} copy(f32[58,16,256]{2,1,0:T(8,128)S(1)} %bitcast.12) | data formatting | bytes 1900544
  75.1 0.9 %copy.24 = f32[58,16,256]{2,1,0:T(8,128)} copy(f32[58,16,256]{2,1,0:T(8,128)S(1)} %bitcast.11) | data formatting | bytes 1900544
  76.0 0.6 copy.25
Async XLA Ops:
  0.6 0.7 copy-start.5
  0.6 0.7 copy-start.6
  0.7 0.7 copy-start.7
  0.7 0.7 copy-start.8
  1.3 1.2 %copy-start = (f32[58,16,256]{2,1,0:T(8,128)S(1)}, f32[58,16,256]{2,1,0:T(8,128)}, u32[]{:S(2)}) copy-start(f32[58,16,256]{2,1,0:T(8,128)} %param.11) | copy-start | bytes 2850820
  2.5 1.2 %copy-start.1 = (f32[58,16,256]{2,1,0:T(8,128)S(1)}, f32[58,16,256]{2,1,0:T(8,128)}, u32[]{:S(2)}) copy-start(f32[58,16,256]{2,1,0:T(8,128)} %param.12) | copy-start | bytes 2850820
  3.7 0.8 %copy-start.2 = (f32[3,16,256]{2,1,0:T(8,128)S(1)}, f32[3,16,256]{2,1,0:T(8,128)}, u32[]{:S(2)}) copy-start(f32[3,16,256]{2,1,0:T(8,128)} %edge_weight.1) | copy-start | bytes 147460
  4.5 0.7 copy-start.3
  5.2 0.7 copy-start.4

commit v2 on v1

--- a/solution.py
+++ b/solution.py
@@ -51,6 +51,7 @@
     corner_recv,
     high,
     low,
+    rain_rows,
     rain_send,
     rain_recv,
     in_sem,
@@ -173,7 +174,8 @@
 
     def edge_tile(r, g, dy):
         first = cols - LANES if dy > 0 else 0
-        return grid[r, pl.ds(pl.multiple_of(g * SUB, SUB), SUB), pl.ds(first, LANES)]
+        at = g * SUB if isinstance(g, int) else pl.multiple_of(g * SUB, SUB)
+        return grid[r, pl.ds(at, SUB), pl.ds(first, LANES)]
 
     def pack(q, carry):
         for side, dy in enumerate((1, -1)):
@@ -193,23 +195,19 @@
     send(col_send.at[0], col_recv.at[0], device(0, 1))
     send(col_send.at[1], col_recv.at[1], device(0, -1))
 
-    def pack_corner(g, carry):
-        result = []
-        for (dx, dy), packed in zip(CORNERS, carry):
+    pair = lane // 2
+    for n, (dx, dy) in enumerate(CORNERS):
+        packed = jnp.zeros((SUB, LANES), jnp.float32)
+        for g in range(groups):
             for k in range(2):
                 p = 4 * g + 2 * k
                 moved = edge_tile((rows if dx > 0 else 2) + k, g, dy)
-                moved = pltpu.roll(moved, lax.rem(p + (2 if dy > 0 else 0), LANES), 1)
-                packed = jnp.where(lane // 2 == 2 * g + k, moved, packed)
-            result.append(packed)
-        return tuple(result)
-
-    packed = lax.fori_loop(
-        0, groups, pack_corner, tuple(jnp.zeros((SUB, LANES), jnp.float32) for _ in CORNERS)
-    )
-    for k, (dx, dy) in enumerate(CORNERS):
-        corner_send[k] = packed[k]
-        send(corner_send.at[k], corner_recv.at[k], device(dx, dy))
+                shift = (p + (2 if dy > 0 else 0)) % LANES
+                if shift:
+                    moved = pltpu.roll(moved, shift, 1)
+                packed = jnp.where(pair == p // 2, moved, packed)
+        corner_send[n] = packed
+        send(corner_send.at[n], corner_recv.at[n], device(dx, dy))
     send_rows(2 * pad, pad)
 
     loads[4 * halves + 2].wait()
@@ -291,13 +289,9 @@
         for k in range(7):
             coef[r, k] = c[k]
 
-        def step(q, carry):
-            for k in range(2):
-                at = pl.ds(pl.multiple_of((q * 2 + k) * SUB, SUB), SUB)
-                lap[r, at, :] = laplace_at(grid, r, at, c)
-            return carry
-
-        lax.fori_loop(0, groups // 2, step, 0)
+        for g in range(groups):
+            at = pl.ds(g * SUB, SUB)
+            lap[r, at, :] = laplace_at(grid, r, at, c)
 
     def coefficients(r):
         return tuple(coef[r, k] for k in range(7))
@@ -307,9 +301,9 @@
         return jnp.concatenate([tile] * halves, axis=1)
 
     def damped(f, r, q, c):
-        at = pl.ds(pl.multiple_of(f * pad + q * SUB, SUB), SUB)
+        at = pl.ds(f * pad + q * SUB, SUB)
         del4 = laplace_at(lap, r, at, c)[:, :cols]
-        here = pl.ds(pl.multiple_of(q * SUB, SUB), SUB)
+        here = pl.ds(q * SUB, SUB)
         return grid[r, at, pl.ds(0, cols)] - spread(f, here) * del4
 
     def put(k, r, q, value):
@@ -321,8 +315,9 @@
     def physics(r):
         c = coefficients(r)
 
-        def step(q, rain):
-            here = pl.ds(pl.multiple_of(q * SUB, SUB), SUB)
+        rain = jnp.zeros((SUB, cols), jnp.float32)
+        for q in range(pad // SUB):
+            here = pl.ds(q * SUB, SUB)
             theta_dyn = damped(0, r, q, c)
             vapor_dyn = damped(1, r, q, c)
             cloud_now = jnp.concatenate(
@@ -346,58 +341,61 @@
             liquid = cloud_now + condensed
             rained = AUTO_RATE * jnp.maximum(liquid - QCRIT, 0.0)
             put(2, r, q, liquid - rained)
-            return rain + spread(5, here) * rained
-
-        rain = lax.fori_loop(0, pad // SUB, step, jnp.zeros((SUB, cols), jnp.float32))
-        total = jnp.sum(rain, axis=0, keepdims=True)
-        place = lax.rem(spans[pl.ds(r - 2, 1), :], LANES)
-        rank = lax.broadcasted_iota(jnp.int32, (LANES, cols), 0)
+            rain = rain + spread(5, here) * rained
+        rain_rows[r - 2] = rain
+
+    rank_low = lax.broadcasted_iota(jnp.int32, (LANES, cols), 0)
+
+    def lower(i):
+        total = jnp.sum(rain_rows[i], axis=0, keepdims=True)
+        place = lax.rem(spans[pl.ds(i, 1), :], LANES)
         head = total.astype(jnp.bfloat16).astype(jnp.float32)
-        at = pl.ds(pl.multiple_of((r - 2) * cols, cols), cols)
+        at = pl.ds(pl.multiple_of(i * cols, cols), cols)
+        hit = rank_low == place
         for k, piece in enumerate((head, total - head)):
-            low[pl.ds(k * LANES, LANES), at] = jnp.where(rank == place, piece, 0.0).astype(
-                jnp.bfloat16
-            )
-
-    def loop(lower, upper_end, do):
+            low[pl.ds(k * LANES, LANES), at] = jnp.where(hit, piece, 0.0).astype(jnp.bfloat16)
+
+    def product(first, count):
+        at = pl.ds(first * cols, count * cols)
+        both = lax.dot_general(
+            high[:, at], low[:, at], (((1,), (1,)), ((), ())), preferred_element_type=jnp.float32
+        )
+        return both[:, :LANES] + both[:, LANES:]
+
+    def loop(first, end, do):
         def step(r, carry):
             do(r)
             return carry
 
-        lax.fori_loop(lower, upper_end, step, 0)
+        lax.fori_loop(first, end, step, 0)
 
     loop(3, rows + 1, first_laplace)
     for h in range(halves):
         loads[3 * halves + h].wait()
     loop(4, rows, physics)
+    loop(2, rows - 2, lower)
+    rain_send[...] = product(2, rows - 4)
 
     for k in (0, 1, 4, 5, 6, 7, 8, 9):
         sends[k].wait_recv()
 
-    def unpack_corner(g, carry):
-        at = pl.ds(pl.multiple_of(g * SUB, SUB), SUB)
-        for dx in (1, -1):
+    for dx in (1, -1):
+        for g in range(groups):
             for k in range(2):
                 p = 4 * g + 2 * k
                 left = corner_recv[CORNERS.index((dx, 1))]
                 right = corner_recv[CORNERS.index((dx, -1))]
-                left = pltpu.roll(left, lax.rem(2 * LANES - 2 - p, LANES), 1)
-                right = pltpu.roll(right, lax.rem(LANES - p, LANES), 1)
+                left = pltpu.roll(left, (LANES - 2 - p) % LANES, 1) if p != LANES - 2 else left
+                right = pltpu.roll(right, LANES - p, 1) if p else right
                 r = k if dx > 0 else rows + 2 + k
-                grid[r, at, pl.ds(cols, LANES)] = jnp.where(lane < 64, right, left)
-        return carry
-
-    lax.fori_loop(0, groups, unpack_corner, 0)
+                grid[r, pl.ds(g * SUB, SUB), pl.ds(cols, LANES)] = jnp.where(lane < 64, right, left)
     loop(0, 4, lambda n: first_laplace(n + 1 + n // 2 * (rows - 2)))
     loop(0, 4, lambda n: physics(n + 2 + n // 2 * (rows - 4)))
 
-    both = lax.dot_general(
-        high[...],
-        low[...],
-        (((1,), (1,)), ((), ())),
-        preferred_element_type=jnp.float32,
-    )
-    rain_send[...] = both[:, :LANES] + both[:, LANES:]
+    for i in (0, 1, rows - 2, rows - 1):
+        lower(i)
+
+    rain_send[...] += product(0, 2) + product(rows - 2, 2)
     rains = []
     for d in range(1, n_py):
         to = device(0, d)
@@ -430,12 +428,8 @@
 
     def diverge(r):
         c = coefficients(r)
-
-        def step(q, carry):
+        for q in range(pad // SUB):
             put(3, r, q, damped(2, r, q, c))
-            return carry
-
-        lax.fori_loop(0, pad // SUB, step, 0)
 
     loop(2, rows + 2, diverge)
     store(3, divergence_out)
@@ -498,6 +492,7 @@
             pltpu.VMEM((4, SUB, LANES), f32),
             pltpu.VMEM((n_py * block, rows * cols), jnp.bfloat16),
             pltpu.VMEM((2 * LANES, rows * cols), jnp.bfloat16),
+            pltpu.VMEM((rows, SUB, cols), f32),
             pltpu.VMEM((n_py * block, LANES), f32),
             pltpu.VMEM((n_py - 1, block, LANES), f32),
             pltpu.SemaphoreType.DMA((4 * halves + 3,)),
@@ -508,7 +503,7 @@
             pltpu.SemaphoreType.DMA((n_py - 1,)),
         ],
         compiler_params=pltpu.CompilerParams(
-            collective_id=0, has_side_effects=True, vmem_limit_bytes=48 * 1024 * 1024
+            collective_id=0, has_side_effects=True, vmem_limit_bytes=60 * 1024 * 1024
         ),
         cost_estimate=pl.CostEstimate(
             flops=60 * levels * rows * cols, bytes_accessed=32 * levels * rows * cols, transcendentals=0

time: 77.1 us -> 40.5 us (0.53)
  Pallas kernels: 66.3 us -> 32.7 us
  local copies, waits for them, and re-layouts: 9.62 us -> 6.88 us
    pallas_call x1, Pallas kernels: 66.3 us -> 32.7 us  [on_device(): pl.pallas_call(functools.partial(kernel, (n_px, n_py, levels, rows, cols)...]
    unnamed x23 -> x13, local copies, waits for them, and re-layouts: 9.62 us -> 6.88 us
where the time goes in v2:
time: 40.5 us; the launch traced here: 40.3 us
  Pallas kernels  32.7 us (81%)
  local copies, waits for them, and re-layouts  6.88 us (17%)
  between operations  0.66 us (2%)
    pallas_call x1, Pallas kernels, on_device(): pl.pallas_call(functools.partial(kernel, (n_px, n_py, levels, rows, cols)...  32.7 us
    unnamed x13, local copies, waits for them, and re-layouts  6.88 us

profile of v2, /device:TPU:0, one launch (start us, length us, event | category | flops | bytes accessed | tf_op | source)
XLA Modules:
  0.0 40.3 jit_solution(9075790159791065473)
XLA Ops:
  0.6 32.7 %shard_map.146 = (f32[928,256]{1,0:T(8,128)}, f32[928,256]{1,0:T(8,128)}, f32[928,256]{1,0:T(8,128)}, f32[928,256]{1,0:T(8,128)}, f32[32,128]{1,0:T(8,128)}) custom-call(f32[928,256]{1,0:T(8,128)} %bitcast.9, f32[928,256]{1,0:T(8,128)} %bitcast.10, f32[928,256]{1,0:T(8,128)} %bitcast.11, f32[928,256]{1,0:T(8,128)} %bitcast.12, f32[3,16,256]{2,1,0:T(8,128)} %edge_weight.1, ...), custom_call_target="tpu_custom_call" | custom-call | flops 14254080 | bytes 7602176 | tf_op jit(solution)/shard_map/pallas_call | solution.py:474
  33.4 0.0 copy-start.2
  33.4 2.3 %copy.21 = f32[58,16,256]{2,1,0:T(8,128)} copy(f32[58,16,256]{2,1,0:T(8,128)} %bitcast.16) | data formatting | bytes 1900544
  35.6 0.0 copy-done.2
  35.7 0.0 copy-start.1
  35.7 0.9 %copy.22 = f32[58,16,256]{2,1,0:T(8,128)} copy(f32[58,16,256]{2,1,0:T(8,128)S(1)} %bitcast.15) | data formatting | bytes 1900544
  36.6 0.6 %copy-done.1 = f32[928,256]{1,0:T(8,128)S(1)} copy-done((f32[928,256]{1,0:T(8,128)S(1)}, f32[928,256]{1,0:T(8,128)}, u32[]{:S(2)}) %copy-start.1) | copy-done | bytes 950296
  37.2 0.0 copy-start
  37.2 0.9 %copy.23 = f32[58,16,256]{2,1,0:T(8,128)} copy(f32[58,16,256]{2,1,0:T(8,128)S(1)} %bitcast.14) | data formatting | bytes 1900544
  38.1 0.6 %copy-done = f32[928,256]{1,0:T(8,128)S(1)} copy-done((f32[928,256]{1,0:T(8,128)S(1)}, f32[928,256]{1,0:T(8,128)}, u32[]{:S(2)}) %copy-start) | copy-done | bytes 950296
  38.7 0.0 copy-start.3
  38.7 0.9 %copy.24 = f32[58,16,256]{2,1,0:T(8,128)} copy(f32[58,16,256]{2,1,0:T(8,128)S(1)} %bitcast.13) | data formatting | bytes 1900544
  39.7 0.0 copy-done.3
  39.7 0.6 %copy.25 = f32[1,4096]{1,0:T(1,128)} copy(f32[1,4096]{1,0:T(1,128)S(1)} %bitcast.17) | data formatting | bytes 32768
Async XLA Ops:
  33.4 2.3 %copy-start.2 = (f32[928,256]{1,0:T(8,128)S(1)}, f32[928,256]{1,0:T(8,128)}, u32[]{:S(2)}) copy-start(f32[928,256]{1,0:T(8,128)} %get-tuple-element.11) | copy-start | bytes 2850820
  35.7 1.5 %copy-start.1 = (f32[928,256]{1,0:T(8,128)S(1)}, f32[928,256]{1,0:T(8,128)}, u32[]{:S(2)}) copy-start(f32[928,256]{1,0:T(8,128)} %get-tuple-element.12) | copy-start | bytes 2850820
  37.2 1.5 %copy-start = (f32[928,256]{1,0:T(8,128)S(1)}, f32[928,256]{1,0:T(8,128)}, u32[]{:S(2)}) copy-start(f32[928,256]{1,0:T(8,128)} %get-tuple-element.13) | copy-start | bytes 2850820
  38.7 0.9 %copy-start.3 = (f32[32,128]{1,0:T(8,128)S(1)}, f32[32,128]{1,0:T(8,128)}, u32[]{:S(2)}) copy-start(f32[32,128]{1,0:T(8,128)} %get-tuple-element.14) | copy-start | bytes 49156

commit v3 on v2

--- a/solution.py
+++ b/solution.py
@@ -75,6 +75,8 @@
         return (lax.rem(px + dx + n_px, n_px), lax.rem(py + dy + n_py, n_py))
 
     loads = []
+    for source, target in ((span_of, spans), (edge_weight, weights), (inv_area, areas)):
+        loads.append(pltpu.make_async_copy(source, target, in_sem.at[len(loads)]))
     for f, source in enumerate((theta, vapor, divergence, cloud)):
         for h in range(halves):
             loads.append(
@@ -84,8 +86,6 @@
                     in_sem.at[len(loads)],
                 )
             )
-    for source, target in ((edge_weight, weights), (inv_area, areas), (span_of, spans)):
-        loads.append(pltpu.make_async_copy(source, target, in_sem.at[len(loads)]))
     for load in loads:
         load.start()
 
@@ -116,8 +116,20 @@
                 ((pad - levels) * rows, LANES), jnp.float32
             )
 
-    for k in list(range(3 * halves)) + [4 * halves, 4 * halves + 1]:
-        loads[k].wait()
+    loads[0].wait()
+    high_count = high.shape[0]
+
+    def upper(i, carry):
+        place = spans[pl.ds(i, 1), :] // LANES
+        rank = lax.broadcasted_iota(jnp.int32, (high_count, cols), 0)
+        hit = jnp.where(rank == place, 1.0, 0.0).astype(jnp.bfloat16)
+        high[:, pl.ds(pl.multiple_of(i * cols, cols), cols)] = hit
+        return carry
+
+    lax.fori_loop(0, rows, upper, 0)
+
+    for load in loads[1 : 3 + 3 * halves]:
+        load.wait()
 
     def turn(i):
         for f in range(3):
@@ -209,18 +221,6 @@
         corner_send[n] = packed
         send(corner_send.at[n], corner_recv.at[n], device(dx, dy))
     send_rows(2 * pad, pad)
-
-    loads[4 * halves + 2].wait()
-    high_count = high.shape[0]
-
-    def upper(i, carry):
-        place = spans[pl.ds(i, 1), :] // LANES
-        rank = lax.broadcasted_iota(jnp.int32, (high_count, cols), 0)
-        hit = jnp.where(rank == place, 1.0, 0.0).astype(jnp.bfloat16)
-        high[:, pl.ds(pl.multiple_of(i * cols, cols), cols)] = hit
-        return carry
-
-    lax.fori_loop(0, rows, upper, 0)
 
     sends[2].wait_recv()
     sends[3].wait_recv()
@@ -289,7 +289,7 @@
         for k in range(7):
             coef[r, k] = c[k]
 
-        for g in range(groups):
+        for g in range(2 * pad // SUB):
             at = pl.ds(g * SUB, SUB)
             lap[r, at, :] = laplace_at(grid, r, at, c)
 
@@ -371,12 +371,17 @@
 
     loop(3, rows + 1, first_laplace)
     for h in range(halves):
-        loads[3 * halves + h].wait()
+        loads[3 + 3 * halves + h].wait()
     loop(4, rows, physics)
-    loop(2, rows - 2, lower)
+
+    def lower_four(n):
+        for k in range(4):
+            lower(2 + 4 * n + k)
+
+    loop(0, (rows - 4) // 4, lower_four)
     rain_send[...] = product(2, rows - 4)
 
-    for k in (0, 1, 4, 5, 6, 7, 8, 9):
+    for k in (0, 1, 4, 5, 6, 7):
         sends[k].wait_recv()
 
     for dx in (1, -1):
@@ -426,12 +431,24 @@
     store(1, vapor_out)
     store(2, cloud_out)
 
-    def diverge(r):
-        c = coefficients(r)
-        for q in range(pad // SUB):
-            put(3, r, q, damped(2, r, q, c))
-
-    loop(2, rows + 2, diverge)
+    for k in (8, 9):
+        sends[k].wait_recv()
+
+    def diverge_first(n):
+        for r in (1 + 2 * n, 2 + 2 * n):
+            c = coefficients(r)
+            for g in range(2 * pad // SUB, groups):
+                at = pl.ds(g * SUB, SUB)
+                lap[r, at, :] = laplace_at(grid, r, at, c)
+
+    def diverge(n):
+        for r in (2 + 2 * n, 3 + 2 * n):
+            c = coefficients(r)
+            for q in range(pad // SUB):
+                put(3, r, q, damped(2, r, q, c))
+
+    loop(0, rows // 2 + 1, diverge_first)
+    loop(0, rows // 2, diverge)
     store(3, divergence_out)
 
     total = rain_send[pl.ds(pl.multiple_of(py * block, block), block), :]
@@ -444,6 +461,23 @@
     for copy in rains:
         copy.wait_send()
     for copy in stores:
+        copy.wait()
+
+
+def placing(*refs):
+    count = len(refs) // 2
+    sem = refs[-1]
+    copies = []
+    for k in range(count):
+        half = refs[k].shape[0] // 2
+        for part in range(2):
+            at = pl.ds(part * half, half)
+            copies.append(
+                pltpu.make_async_copy(refs[k].at[at], refs[count + k].at[at], sem.at[k, part])
+            )
+    for copy in copies:
+        copy.start()
+    for copy in copies:
         copy.wait()
 
 
@@ -470,11 +504,12 @@
     flat = jax.ShapeDtypeStruct((levels * rows, cols), jnp.float32)
     f32 = jnp.float32
     anywhere = pl.BlockSpec(memory_space=pl.ANY)
+    far = pl.BlockSpec(memory_space=pltpu.HBM)
     scalars = pl.BlockSpec(memory_space=pltpu.SMEM)
-    theta_next, vapor_next, cloud_next, divergence_next, precip = pl.pallas_call(
+    made = pl.pallas_call(
         functools.partial(kernel, (n_px, n_py, levels, rows, cols)),
         out_shape=(flat, flat, flat, flat, jax.ShapeDtypeStruct((block, LANES), f32)),
-        in_specs=[anywhere] * 7 + [scalars] * 4,
+        in_specs=[far] * 7 + [scalars] * 4,
         out_specs=(anywhere,) * 4 + (pl.BlockSpec(memory_space=pltpu.VMEM),),
         scratch_shapes=[
             pltpu.VMEM((4, halves, pad * rows, LANES), f32),
@@ -503,25 +538,37 @@
             pltpu.SemaphoreType.DMA((n_py - 1,)),
         ],
         compiler_params=pltpu.CompilerParams(
-            collective_id=0, has_side_effects=True, vmem_limit_bytes=60 * 1024 * 1024
+            collective_id=0, has_side_effects=True, vmem_limit_bytes=40 * 1024 * 1024
         ),
         cost_estimate=pl.CostEstimate(
             flops=60 * levels * rows * cols, bytes_accessed=32 * levels * rows * cols, transcendentals=0
         ),
     )(
-        theta.reshape(levels * rows, cols),
-        vapor.reshape(levels * rows, cols),
-        divergence.reshape(levels * rows, cols),
-        cloud.reshape(levels * rows, cols),
-        edge_weight,
-        inv_area,
-        span_of,
+        *[
+            pltpu.with_memory_space_constraint(array, pltpu.HBM)
+            for array in (
+                theta.reshape(levels * rows, cols),
+                vapor.reshape(levels * rows, cols),
+                divergence.reshape(levels * rows, cols),
+                cloud.reshape(levels * rows, cols),
+                edge_weight,
+                inv_area,
+                span_of,
+            )
+        ],
         damping,
         exner,
         sat_scale,
         layer_mass,
     )
     shape = (levels, rows, cols)
+    theta_next, vapor_next, cloud_next, divergence_next, precip = pl.pallas_call(
+        placing,
+        out_shape=tuple(jax.ShapeDtypeStruct(array.shape, array.dtype) for array in made),
+        in_specs=[anywhere] * 5,
+        out_specs=(far,) * 5,
+        scratch_shapes=[pltpu.SemaphoreType.DMA((len(made), 2))],
+    )(*made)
     return (
         theta_next.reshape(shape),
         vapor_next.reshape(shape),

time: 40.5 us -> 154 us (3.80)
  Pallas kernels: 32.7 us -> 148 us
  local copies, waits for them, and re-layouts: 6.88 us -> 5.09 us
    pallas_call x0 -> x1, Pallas kernels: none -> 117 us  [on_device(): pl.pallas_call(placing, out_shape=tuple((jax.ShapeDtypeStruct(array.shape...]
    unnamed x13 -> x18, local copies, waits for them, and re-layouts: 6.88 us -> 5.09 us
    pallas_call x1, Pallas kernels: 32.7 us -> 31.1 us  [on_device(): pl.pallas_call(functools.partial(kernel, (n_px, n_py, levels, rows, cols)...]
where the time goes in v3:
time: 154 us
  Pallas kernels  148 us (96%)
  local copies, waits for them, and re-layouts  5.09 us (3%)
    pallas_call x1, Pallas kernels, on_device(): pl.pallas_call(placing, out_shape=tuple((jax.ShapeDtypeStruct(array.shape...  117 us
    pallas_call x1, Pallas kernels, on_device(): pl.pallas_call(functools.partial(kernel, (n_px, n_py, levels, rows, cols)...  31.1 us
    unnamed x18, local copies, waits for them, and re-layouts  5.09 us

profile of v3, /device:TPU:0, one launch (start us, length us, event | category | flops | bytes accessed | tf_op | source)
XLA Modules:
  0.0 153.7 jit_solution(5156726089054197175)
XLA Ops:
  0.6 0.0 copy-start.5
  0.6 0.0 copy-start.6
  0.7 0.0 copy-start.7
  0.7 0.0 copy-start.8
  0.7 0.6 copy-done.5
  1.3 0.0 copy-done.6
  1.3 0.0 copy-done.7
  1.3 0.0 copy-done.8
  1.3 31.1 %shard_map.146 = (f32[928,256]{1,0:T(8,128)S(1)}, f32[928,256]{1,0:T(8,128)S(1)}, f32[928,256]{1,0:T(8,128)S(1)}, f32[928,256]{1,0:T(8,128)S(1)}, f32[32,128]{1,0:T(8,128)S(1)}) custom-call(f32[928,256]{1,0:T(8,128)} %bitcast.9, f32[928,256]{1,0:T(8,128)} %bitcast.10, f32[928,256]{1,0:T(8,128)} %bitcast.11, f32[928,256]{1,0:T(8,128)} %bitcast.12, ...), custom_call_target="tpu_custom_call" | custom-call | flops 14254080 | bytes 7602176 | tf_op jit(solution)/shard_map/pallas_call | solution.py:509
  32.5 0.0 copy-start
  32.5 0.9 copy-done
  33.4 0.0 copy-start.1
  33.4 1.0 copy-done.1
  34.4 0.0 copy-start.2
  34.4 0.9 copy-done.2
  35.4 0.0 copy-start.3
  35.4 0.9 copy-done.3
  36.3 0.0 copy-start.4
  36.3 0.6 copy-done.4
  36.9 116.8 %shard_map.147 = (f32[928,256]{1,0:T(8,128)}, f32[928,256]{1,0:T(8,128)}, f32[928,256]{1,0:T(8,128)}, f32[928,256]{1,0:T(8,128)}, f32[32,128]{1,0:T(8,128)}) custom-call(f32[928,256]{1,0:T(8,128)} %copy-done, f32[928,256]{1,0:T(8,128)} %copy-done.1, f32[928,256]{1,0:T(8,128)} %copy-done.2, f32[928,256]{1,0:T(8,128)} %copy-done.3, f32[32,128]{1,0:T(8,128)} %copy-done.4), custom_call_target="tpu_custom_call" | custom-call | tf_op jit(solution)/shard_map/pallas_call | solution.py:565
Async XLA Ops:
  0.6 0.7 copy-start.5
  0.6 0.7 copy-start.6
  0.7 0.7 copy-start.7
  0.7 0.7 copy-start.8
  32.5 0.9 copy-start
  33.4 1.0 copy-start.1
  34.4 1.0 copy-start.2
  35.4 0.9 copy-start.3
  36.3 0.6 copy-start.4

commit v4 on v3

--- a/solution.py
+++ b/solution.py
@@ -334,7 +334,10 @@
                 warmed = temper + LATENT * condensed if repeat else temper
                 saturation = scale * jnp.exp(warmed)
                 excess = vapor_dyn - condensed - saturation
-                condensed = condensed + excess / (1.0 + LATENT * saturation)
+                slope = 1.0 + LATENT * saturation
+                inverse = pl.reciprocal(slope, approx=True)
+                inverse = inverse * (2.0 - slope * inverse)
+                condensed = condensed + excess * inverse
             condensed = jnp.maximum(condensed, -cloud_now)
             put(0, r, q, theta_dyn + condensed * spread(6, here))
             put(1, r, q, vapor_dyn - condensed)
@@ -565,10 +568,11 @@
     theta_next, vapor_next, cloud_next, divergence_next, precip = pl.pallas_call(
         placing,
         out_shape=tuple(jax.ShapeDtypeStruct(array.shape, array.dtype) for array in made),
-        in_specs=[anywhere] * 5,
+        in_specs=[pl.BlockSpec(memory_space=pltpu.VMEM)] * 5,
         out_specs=(far,) * 5,
         scratch_shapes=[pltpu.SemaphoreType.DMA((len(made), 2))],
-    )(*made)
+        compiler_params=pltpu.CompilerParams(vmem_limit_bytes=1024 * 1024),
+    )(*[pltpu.with_memory_space_constraint(array, pltpu.VMEM) for array in made])
     return (
         theta_next.reshape(shape),
         vapor_next.reshape(shape),

time: 154 us -> 34.8 us (0.23)
  Pallas kernels: 148 us -> 33.2 us
  local copies, waits for them, and re-layouts: 5.09 us -> 0.67 us
    pallas_call x1, Pallas kernels: 117 us -> 1.96 us  [on_device(): pl.pallas_call(placing, out_shape=tuple((jax.ShapeDtypeStruct(array.shape...]
    unnamed x18 -> x8, local copies, waits for them, and re-layouts: 5.09 us -> 0.67 us
where the time goes in v4:
time: 34.8 us; the launch traced here: 34.5 us
  Pallas kernels  33.2 us (95%)
  between operations  0.68 us (2%)
  local copies, waits for them, and re-layouts  0.67 us (2%)
    pallas_call x1, Pallas kernels, on_device(): pl.pallas_call(functools.partial(kernel, (n_px, n_py, levels, rows, cols)...  31.2 us
    pallas_call x1, Pallas kernels, on_device(): pl.pallas_call(placing, out_shape=tuple((jax.ShapeDtypeStruct(array.shape...  1.96 us

profile of v4, /device:TPU:0, one launch (start us, length us, event | category | flops | bytes accessed | tf_op | source)
XLA Modules:
  0.0 34.5 jit_solution(2492175871139759765)
XLA Ops:
  0.6 0.0 copy-start
  0.6 0.0 copy-start.1
  0.7 0.0 copy-start.2
  0.7 0.0 copy-start.3
  0.7 0.6 %copy-done = f32[3,58]{1,0:T(4,128)S(1)} copy-done((f32[3,58]{1,0:T(4,128)S(1)}, f32[3,58]{1,0:T(4,128)}, u32[]{:S(2)}) %copy-start) | copy-done | bytes 720
  1.3 0.0 copy-done.1
  1.3 0.0 copy-done.2
  1.3 0.0 copy-done.3
  1.3 31.2 %shard_map.146 = (f32[928,256]{1,0:T(8,128)S(1)}, f32[928,256]{1,0:T(8,128)S(1)}, f32[928,256]{1,0:T(8,128)S(1)}, f32[928,256]{1,0:T(8,128)S(1)}, f32[32,128]{1,0:T(8,128)S(1)}) custom-call(f32[928,256]{1,0:T(8,128)} %bitcast.9, f32[928,256]{1,0:T(8,128)} %bitcast.10, f32[928,256]{1,0:T(8,128)} %bitcast.11, f32[928,256]{1,0:T(8,128)} %bitcast.12, ...), custom_call_target="tpu_custom_call" | custom-call | flops 14254080 | bytes 7602176 | tf_op jit(solution)/shard_map/pallas_call | solution.py:512
  32.6 2.0 %shard_map.147 = (f32[928,256]{1,0:T(8,128)}, f32[928,256]{1,0:T(8,128)}, f32[928,256]{1,0:T(8,128)}, f32[928,256]{1,0:T(8,128)}, f32[32,128]{1,0:T(8,128)}) custom-call(f32[928,256]{1,0:T(8,128)S(1)} %get-tuple-element.15.refs_0_, f32[928,256]{1,0:T(8,128)S(1)} %get-tuple-element.16.refs_1_, f32[928,256]{1,0:T(8,128)S(1)} %get-tuple-element.17.refs_2_, ...), custom_call_target="tpu_custom_call" | custom-call | tf_op jit(solution)/shard_map/pallas_call | solution.py:568
Async XLA Ops:
  0.6 0.7 %copy-start = (f32[3,58]{1,0:T(4,128)S(1)}, f32[3,58]{1,0:T(4,128)}, u32[]{:S(2)}) copy-start(f32[3,58]{1,0:T(4,128)} %damping.1) | copy-start | bytes 2092
  0.6 0.7 %copy-start.1 = (f32[58]{0:T(128)S(1)}, f32[58]{0:T(128)}, u32[]{:S(2)}) copy-start(f32[58]{0:T(128)} %exner.1) | copy-start | bytes 700
  0.7 0.7 %copy-start.2 = (f32[58]{0:T(128)S(1)}, f32[58]{0:T(128)}, u32[]{:S(2)}) copy-start(f32[58]{0:T(128)} %sat_scale.1) | copy-start | bytes 700
  0.7 0.7 %copy-start.3 = (f32[58]{0:T(128)S(1)}, f32[58]{0:T(128)}, u32[]{:S(2)}) copy-start(f32[58]{0:T(128)} %layer_mass.1) | copy-start | bytes 700

commit v5 on v4

--- a/solution.py
+++ b/solution.py
@@ -38,6 +38,7 @@
     precip_out,
     nat,
     out,
+    made,
     grid,
     lap,
     coef,
@@ -131,21 +132,26 @@
     for load in loads[1 : 3 + 3 * halves]:
         load.wait()
 
-    def turn(i):
+    def turned(f, q, h):
+        block_rows = nat[f, h, pl.ds(pl.multiple_of(q * (SUB * rows), SUB * rows), SUB * rows), :]
+        return jnp.swapaxes(block_rows.reshape(SUB, rows, LANES), 0, 1)
+
+    def turn(q, carry):
         for f in range(3):
             for h in range(halves):
-                grid[i + 2, pl.ds(f * pad, pad), pl.ds(h * LANES, LANES)] = nat[
-                    f, h, pl.ds(i, pad, stride=rows), :
-                ]
+                at = pl.ds(pl.multiple_of(f * pad + q * SUB, SUB), SUB)
+                grid[pl.ds(2, rows), at, pl.ds(h * LANES, LANES)] = turned(f, q, h)
+        return carry
+
+    lax.fori_loop(0, pad // SUB, turn, 0)
+
+    def turn_geometry(i, carry):
         for k in range(3):
             grid[i + 2, pl.ds(levels + k, 1), pl.ds(0, cols)] = weights[k, pl.ds(i, 1), :]
         grid[i + 2, pl.ds(levels + 3, 1), pl.ds(0, cols)] = areas[pl.ds(i, 1), :]
-
-    def turn_edge(n, carry):
-        turn(n + n // 2 * (rows - 4))
         return carry
 
-    lax.fori_loop(0, 4, turn_edge, 0)
+    lax.fori_loop(0, rows, turn_geometry, 0)
     pl.semaphore_wait(barrier, len(greeted))
 
     sends = []
@@ -174,12 +180,6 @@
         )
 
     send_rows(0, 2 * pad)
-
-    def turn_inner(n, carry):
-        turn(n + 2)
-        return carry
-
-    lax.fori_loop(0, rows - 4, turn_inner, 0)
 
     lane = lax.broadcasted_iota(jnp.int32, (SUB, LANES), 1)
     per = LANES // (2 * rows)
@@ -307,10 +307,7 @@
         return grid[r, at, pl.ds(0, cols)] - spread(f, here) * del4
 
     def put(k, r, q, value):
-        for h in range(halves):
-            out[k, h, pl.ds(q * (SUB * rows) + r - 2, SUB, stride=rows), :] = value[
-                :, h * LANES : (h + 1) * LANES
-            ]
+        made[k, r - 2, pl.ds(q * SUB, SUB), :] = value
 
     def physics(r):
         c = coefficients(r)
@@ -320,13 +317,7 @@
             here = pl.ds(q * SUB, SUB)
             theta_dyn = damped(0, r, q, c)
             vapor_dyn = damped(1, r, q, c)
-            cloud_now = jnp.concatenate(
-                [
-                    nat[3, h, pl.ds(q * (SUB * rows) + r - 2, SUB, stride=rows), :]
-                    for h in range(halves)
-                ],
-                axis=1,
-            )
+            cloud_now = made[2, r - 2, here, :]
             temper = theta_dyn * spread(3, here)
             scale = spread(4, here)
             condensed = jnp.zeros_like(temper)
@@ -375,6 +366,14 @@
     loop(3, rows + 1, first_laplace)
     for h in range(halves):
         loads[3 + 3 * halves + h].wait()
+
+    def turn_cloud(q, carry):
+        for h in range(halves):
+            at = pl.ds(pl.multiple_of(q * SUB, SUB), SUB)
+            made[2, :, at, pl.ds(h * LANES, LANES)] = turned(3, q, h)
+        return carry
+
+    lax.fori_loop(0, pad // SUB, turn_cloud, 0)
     loop(4, rows, physics)
 
     def lower_four(n):
@@ -420,7 +419,19 @@
 
     stores = []
 
+    def turn_back(k):
+        def step(q, carry):
+            for h in range(halves):
+                at = pl.ds(pl.multiple_of(q * SUB, SUB), SUB)
+                back = jnp.swapaxes(made[k, :, at, pl.ds(h * LANES, LANES)], 0, 1)
+                to = pl.ds(pl.multiple_of(q * (SUB * rows), SUB * rows), SUB * rows)
+                out[k, h, to, :] = back.reshape(SUB * rows, LANES)
+            return carry
+
+        lax.fori_loop(0, pad // SUB, step, 0)
+
     def store(k, target):
+        turn_back(k)
         for h in range(halves):
             copy = pltpu.make_async_copy(
                 out.at[k, h, pl.ds(0, used), :],
@@ -517,6 +528,7 @@
         scratch_shapes=[
             pltpu.VMEM((4, halves, pad * rows, LANES), f32),
             pltpu.VMEM((4, halves, pad * rows, LANES), f32),
+            pltpu.VMEM((4, rows, pad, cols), f32),
             pltpu.VMEM((rows + 4, 3 * pad, wide), f32),
             pltpu.VMEM((rows + 4, 3 * pad, wide), f32),
             pltpu.VMEM((rows + 4, 7, SUB, wide), f32),

time: 34.8 us -> 32.7 us (0.940)
  Pallas kernels: 33.2 us -> 31.1 us
    pallas_call x1, Pallas kernels: 31.2 us -> 29.1 us  [on_device(): pl.pallas_call(functools.partial(kernel, (n_px, n_py, levels, rows, cols)...]
where the time goes in v5:
time: 32.7 us; the launch traced here: 32.4 us
  Pallas kernels  31.1 us (95%)
  between operations  0.68 us (2%)
  local copies, waits for them, and re-layouts  0.67 us (2%)
    pallas_call x1, Pallas kernels, on_device(): pl.pallas_call(functools.partial(kernel, (n_px, n_py, levels, rows, cols)...  29.1 us
    pallas_call x1, Pallas kernels, on_device(): pl.pallas_call(placing, out_shape=tuple((jax.ShapeDtypeStruct(array.shape...  1.96 us
    unnamed x8, local copies, waits for them, and re-layouts  0.67 us

profile of v5, /device:TPU:0, one launch (start us, length us, event | category | flops | bytes accessed | tf_op | source)
XLA Modules:
  0.0 32.4 jit_solution(6149148575179425644)
XLA Ops:
  0.6 0.0 copy-start
  0.6 0.0 copy-start.1
  0.7 0.0 copy-start.2
  0.7 0.0 copy-start.3
  0.7 0.6 %copy-done = f32[3,58]{1,0:T(4,128)S(1)} copy-done((f32[3,58]{1,0:T(4,128)S(1)}, f32[3,58]{1,0:T(4,128)}, u32[]{:S(2)}) %copy-start) | copy-done | bytes 720
  1.3 0.0 copy-done.1
  1.3 0.0 copy-done.2
  1.3 0.0 copy-done.3
  1.3 29.1 %shard_map.146 = (f32[928,256]{1,0:T(8,128)S(1)}, f32[928,256]{1,0:T(8,128)S(1)}, f32[928,256]{1,0:T(8,128)S(1)}, f32[928,256]{1,0:T(8,128)S(1)}, f32[32,128]{1,0:T(8,128)S(1)}) custom-call(f32[928,256]{1,0:T(8,128)} %bitcast.9, f32[928,256]{1,0:T(8,128)} %bitcast.10, f32[928,256]{1,0:T(8,128)} %bitcast.11, f32[928,256]{1,0:T(8,128)} %bitcast.12, ...), custom_call_target="tpu_custom_call" | custom-call | flops 14254080 | bytes 7602176 | tf_op jit(solution)/shard_map/pallas_call | solution.py:523
  30.5 2.0 %shard_map.147 = (f32[928,256]{1,0:T(8,128)}, f32[928,256]{1,0:T(8,128)}, f32[928,256]{1,0:T(8,128)}, f32[928,256]{1,0:T(8,128)}, f32[32,128]{1,0:T(8,128)}) custom-call(f32[928,256]{1,0:T(8,128)S(1)} %get-tuple-element.15.refs_0_, f32[928,256]{1,0:T(8,128)S(1)} %get-tuple-element.16.refs_1_, f32[928,256]{1,0:T(8,128)S(1)} %get-tuple-element.17.refs_2_, ...), custom_call_target="tpu_custom_call" | custom-call | tf_op jit(solution)/shard_map/pallas_call | solution.py:580
Async XLA Ops:
  0.6 0.7 %copy-start = (f32[3,58]{1,0:T(4,128)S(1)}, f32[3,58]{1,0:T(4,128)}, u32[]{:S(2)}) copy-start(f32[3,58]{1,0:T(4,128)} %damping.1) | copy-start | bytes 2092
  0.6 0.7 %copy-start.1 = (f32[58]{0:T(128)S(1)}, f32[58]{0:T(128)}, u32[]{:S(2)}) copy-start(f32[58]{0:T(128)} %exner.1) | copy-start | bytes 700
  0.7 0.7 %copy-start.2 = (f32[58]{0:T(128)S(1)}, f32[58]{0:T(128)}, u32[]{:S(2)}) copy-start(f32[58]{0:T(128)} %sat_scale.1) | copy-start | bytes 700
  0.7 0.7 %copy-start.3 = (f32[58]{0:T(128)S(1)}, f32[58]{0:T(128)}, u32[]{:S(2)}) copy-start(f32[58]{0:T(128)} %layer_mass.1) | copy-start | bytes 700

commit v6 on v5

--- a/solution.py
+++ b/solution.py
@@ -363,7 +363,14 @@
 
         lax.fori_loop(first, end, step, 0)
 
-    loop(3, rows + 1, first_laplace)
+    def twice(do, first):
+        def step(n):
+            do(first + 2 * n)
+            do(first + 2 * n + 1)
+
+        return step
+
+    loop(0, (rows - 2) // 2, twice(first_laplace, 3))
     for h in range(halves):
         loads[3 + 3 * halves + h].wait()
 
@@ -374,7 +381,7 @@
         return carry
 
     lax.fori_loop(0, pad // SUB, turn_cloud, 0)
-    loop(4, rows, physics)
+    loop(0, (rows - 4) // 2, twice(physics, 4))
 
     def lower_four(n):
         for k in range(4):

time: 32.7 us -> 32.3 us (0.988)
  Pallas kernels: 31.1 us -> 30.7 us
    pallas_call x1, Pallas kernels: 29.1 us -> 28.7 us  [on_device(): pl.pallas_call(functools.partial(kernel, (n_px, n_py, levels, rows, cols)...]
where the time goes in v6:
time: 32.3 us; the launch traced here: 32 us
  Pallas kernels  30.7 us (95%)
  between operations  0.68 us (2%)
  local copies, waits for them, and re-layouts  0.67 us (2%)
    pallas_call x1, Pallas kernels, on_device(): pl.pallas_call(functools.partial(kernel, (n_px, n_py, levels, rows, cols)...  28.7 us
    pallas_call x1, Pallas kernels, on_device(): pl.pallas_call(placing, out_shape=tuple((jax.ShapeDtypeStruct(array.shape...  1.96 us
    unnamed x8, local copies, waits for them, and re-layouts  0.67 us

profile of v6, /device:TPU:0, one launch (start us, length us, event | category | flops | bytes accessed | tf_op | source)
XLA Modules:
  0.0 32.0 jit_solution(5585330829422392599)
XLA Ops:
  0.6 0.0 copy-start
  0.6 0.0 copy-start.1
  0.7 0.0 copy-start.2
  0.7 0.0 copy-start.3
  0.7 0.6 %copy-done = f32[3,58]{1,0:T(4,128)S(1)} copy-done((f32[3,58]{1,0:T(4,128)S(1)}, f32[3,58]{1,0:T(4,128)}, u32[]{:S(2)}) %copy-start) | copy-done | bytes 720
  1.3 0.0 copy-done.1
  1.3 0.0 copy-done.2
  1.3 0.0 copy-done.3
  1.3 28.7 %shard_map.146 = (f32[928,256]{1,0:T(8,128)S(1)}, f32[928,256]{1,0:T(8,128)S(1)}, f32[928,256]{1,0:T(8,128)S(1)}, f32[928,256]{1,0:T(8,128)S(1)}, f32[32,128]{1,0:T(8,128)S(1)}) custom-call(f32[928,256]{1,0:T(8,128)} %bitcast.9, f32[928,256]{1,0:T(8,128)} %bitcast.10, f32[928,256]{1,0:T(8,128)} %bitcast.11, f32[928,256]{1,0:T(8,128)} %bitcast.12, ...), custom_call_target="tpu_custom_call" | custom-call | flops 14254080 | bytes 7602176 | tf_op jit(solution)/shard_map/pallas_call | solution.py:530
  30.1 2.0 %shard_map.147 = (f32[928,256]{1,0:T(8,128)}, f32[928,256]{1,0:T(8,128)}, f32[928,256]{1,0:T(8,128)}, f32[928,256]{1,0:T(8,128)}, f32[32,128]{1,0:T(8,128)}) custom-call(f32[928,256]{1,0:T(8,128)S(1)} %get-tuple-element.15.refs_0_, f32[928,256]{1,0:T(8,128)S(1)} %get-tuple-element.16.refs_1_, f32[928,256]{1,0:T(8,128)S(1)} %get-tuple-element.17.refs_2_, ...), custom_call_target="tpu_custom_call" | custom-call | tf_op jit(solution)/shard_map/pallas_call | solution.py:587
Async XLA Ops:
  0.6 0.7 %copy-start = (f32[3,58]{1,0:T(4,128)S(1)}, f32[3,58]{1,0:T(4,128)}, u32[]{:S(2)}) copy-start(f32[3,58]{1,0:T(4,128)} %damping.1) | copy-start | bytes 2092
  0.6 0.7 %copy-start.1 = (f32[58]{0:T(128)S(1)}, f32[58]{0:T(128)}, u32[]{:S(2)}) copy-start(f32[58]{0:T(128)} %exner.1) | copy-start | bytes 700
  0.7 0.7 %copy-start.2 = (f32[58]{0:T(128)S(1)}, f32[58]{0:T(128)}, u32[]{:S(2)}) copy-start(f32[58]{0:T(128)} %sat_scale.1) | copy-start | bytes 700
  0.7 0.7 %copy-start.3 = (f32[58]{0:T(128)S(1)}, f32[58]{0:T(128)}, u32[]{:S(2)}) copy-start(f32[58]{0:T(128)} %layer_mass.1) | copy-start | bytes 700
